TPU v7x, 256 devices: a whole 4x4x8 slice. The times are simulated.
256 devices in a mesh: dp: 8 (over x_lo, y), tensor: 32 (over z, x_hi, core).
Axes of the slice: x: 4 (x_hi: 2, x_lo: 2; x = x_hi * 2 + x_lo), y: 4, z: 8, core: 2. Of those that a mesh axis runs over, the one named last changes fastest.
Arguments:
- hidden: bfloat16 [1024, 53248], P('dp', 'tensor'), may hold values from -0.29882812 to 0.29882812
- upstream: bfloat16 [1024, 8192], P('dp'), may hold values from -6 to 6
- weight: bfloat16 [53248, 8192], P('tensor', 'dp'), may hold values from -0.0625 to 0.0625
- scales: float32 [416, 8192], P('tensor', 'dp'), may hold values from 0.3 to 3
- clip_mask: int32 [416, 8192], P('tensor', 'dp'), may hold values 0 or 1
- rot_block: float32 [13, 13], replicated, may hold values from -1.75 to 1.75
Outputs:
- grad_hidden: bfloat16 [1024, 53248], P('dp', 'tensor')
- grad_weight: bfloat16 [53248, 8192], P('tensor', 'dp')
- grad_scales: float32 [416, 8192], P('tensor', 'dp')
All inputs are finite; a program needn't handle non-finite values. No bound on the sum of `clip_mask` on one device may be relied on, other than what follows from the above.
Results may differ from a plain program's by a relative error of at most 0.023.
Values may be sent and summed in bfloat16 or wider, within the bound.
A program may use at most 192 MiB of HBM per device.

v0:
```python
import jax
import jax.numpy as jnp
from jax import lax
from jax.sharding import PartitionSpec as P

HB = 128
GROUP = 128


def sign_table(size):
    index = jnp.arange(size, dtype=jnp.int32)
    both = index[:, None] & index[None, :]
    parity = jnp.zeros((size, size), jnp.int32)
    for shift_bit in range(max(size.bit_length() - 1, 0)):
        parity = parity ^ both >> shift_bit & 1
    return 1.0 - 2.0 * parity.astype(jnp.float32)


def local_forward(values, rot_block):
    rows, width = values.shape
    blocks = rot_block.shape[0]
    inner = sign_table(HB).astype(jnp.bfloat16)
    first = jnp.dot(values.reshape(rows * blocks, HB), inner, preferred_element_type=jnp.float32)
    first = first.reshape(rows, blocks, HB)
    mixed = jnp.einsum("nkd,kc->ncd", first, rot_block, precision=lax.Precision.HIGHEST) * HB ** (
        -0.5
    )
    return mixed.reshape(rows, width).astype(jnp.bfloat16)


def local_backward(values, rot_block):
    rows, width = values.shape
    blocks = rot_block.shape[0]
    inner = sign_table(HB).astype(jnp.bfloat16)
    first = jnp.dot(values.reshape(rows * blocks, HB), inner, preferred_element_type=jnp.float32)
    first = first.reshape(rows, blocks, HB)
    mixed = jnp.einsum("ncb,kc->nkb", first, rot_block, precision=lax.Precision.HIGHEST) * HB ** (
        -0.5
    )
    return mixed.reshape(rows, width).astype(jnp.bfloat16)


def cross_apply(values):
    rows, width = values.shape
    size = lax.axis_size("tensor")
    table = sign_table(size)
    summed = jnp.einsum(
        "nsf,st->ntf",
        lax.all_to_all(
            values.reshape(rows, 1, width), "tensor", split_axis=0, concat_axis=1, tiled=True
        ).astype(jnp.float32),
        table,
        precision=lax.Precision.HIGHEST,
    )
    summed = (summed * size ** (-0.5)).astype(jnp.bfloat16)
    result = lax.all_to_all(summed, "tensor", split_axis=1, concat_axis=0, tiled=True)
    return result.reshape(rows, width)


def shards(hidden, upstream, weight, scales, clip_mask, rot_block):
    rows, width = hidden.shape
    groups, cols = scales.shape
    rotated = cross_apply(local_forward(hidden, rot_block))
    moved = lax.all_to_all(upstream, "dp", split_axis=1, concat_axis=0, tiled=True)
    part = moved
    grad = lax.dot_general(
        lax.all_gather(rotated, "dp", axis=0, tiled=True),
        part,
        (((0,), (0,)), ((), ())),
        preferred_element_type=jnp.float32,
    )
    w_wide = weight.astype(jnp.float32).reshape(groups, GROUP, cols)
    grad_groups = grad.reshape(groups, GROUP, cols)
    grad_weight = (
        (clip_mask.astype(jnp.float32)[:, None, :] * scales[:, None, :] * grad_groups)
        .reshape(width, cols)
        .astype(jnp.bfloat16)
    )
    grad_scales = jnp.sum(grad_groups * w_wide, axis=1)
    quant = (w_wide * scales[:, None, :]).reshape(width, cols).astype(jnp.bfloat16)
    part = moved
    summed = lax.psum_scatter(
        lax.dot_general(
            part, quant, (((1,), (1,)), ((), ())), preferred_element_type=jnp.float32
        ).astype(jnp.bfloat16),
        "dp",
        scatter_dimension=0,
        tiled=True,
    )
    grad_mixed = cross_apply(summed)
    grad_hidden = local_backward(grad_mixed, rot_block)
    return (grad_hidden, grad_weight, grad_scales)


def solution(mesh):
    return jax.shard_map(
        shards,
        mesh=mesh,
        in_specs=(
            P("dp", "tensor"),
            P("dp", None),
            P("tensor", "dp"),
            P("tensor", "dp"),
            P("tensor", "dp"),
            P(),
        ),
        out_specs=(P("dp", "tensor"), P("tensor", "dp"), P("tensor", "dp")),
        check_vma=False,
    )
```

profile of v0, /device:TPU:1, one launch (start us, length us, event | category | flops | bytes accessed | tf_op | source)
XLA Modules:
  0.0 216.2 jit_solution(16601340837875472558)
XLA Ops:
  7.2 3.3 %copy.61 = bf16[16,8,8,1024]{3,2,0,1:T(8,128)(2,1)} copy(bf16[16,8,8,1024]{3,2,1,0:T(8,128)(2,1)} %bitcast.77) | data formatting | bytes 4194304 | tf_op jit(solution)/shard_map/all_to_all | solution.py:64
  10.5 5.9 %all-to-all-start = ((bf16[128,8,1024]{2,0,1:T(8,128)(2,1)}), bf16[128,8,1024]{2,0,1:T(8,128)(2,1)}, u32[]{:S(2)}, u32[]{:S(2)}) async-start(bf16[128,8,1024]{2,0,1:T(8,128)(2,1)} %bitcast.73), calls=%async_computation | async-start | bytes 4194304 | tf_op jit(solution)/shard_map/all_to_all | solution.py:64
  16.5 2.8 %fusion = bf16[1664,1024]{1,0:T(8,128)(2,1)} fusion(f32[13,1024]{1,0:T(8,128)S(1)} %copy-done.4, bf16[1664,1024]{1,0:T(8,128)(2,1)S(1)} %copy-done.1), kind=kLoop, calls=%fused_computation.1 | loop fusion | flops 5111808 | bytes 6868992 | tf_op jit(solution)/shard_map/convert_element_type | solution.py:80
  19.3 23.4 %all-to-all-done = bf16[128,8,1024]{2,0,1:T(8,128)(2,1)} async-done(((bf16[128,8,1024]{2,0,1:T(8,128)(2,1)}), bf16[128,8,1024]{2,0,1:T(8,128)(2,1)}, u32[]{:S(2)}, u32[]{:S(2)}) %all-to-all-start) | async-done | bytes 2097184 | tf_op jit(solution)/shard_map/all_to_all | solution.py:64
  42.7 6.4 %fusion.1 = bf16[1024,1664]{0,1:T(8,128)(2,1)S(1)} fusion(bf16[1664,1024]{1,0:T(8,128)(2,1)} %fusion, bf16[1024,1024]{1,0:T(8,128)(2,1)} %bitcast.3), kind=kOutput, calls=%fused_computation.5 | convolution fusion | flops 3491364864 | bytes 8912896 | tf_op jit(solution)/shard_map/dot_general | solution.py:83
  49.1 3.5 %copy.43 = bf16[1024,1664]{1,0:T(8,128)(2,1)} copy(bf16[1024,1664]{0,1:T(8,128)(2,1)S(1)} %fusion.1) | data formatting | bytes 6815744
  52.7 0.9 copy-done.3
  53.6 0.5 reshape.54
  54.8 1.0 fusion.8
  56.3 0.5 broadcast.181
  56.8 0.9 reduce.3
  58.3 26.4 %all_to_all.85 = bf16[32,2,3328]{2,1,0:T(2,128)(2,1)S(1)} all-to-all(bf16[32,2,3328]{2,1,0:T(2,128)(2,1)S(1)} %reshape.69), channel_id=1, replica_groups=mesh['dp'=8,'tensor'=32] {'tensor'}, dimensions={0} | all-to-all | bytes 851968 | tf_op jit(solution)/shard_map/all_to_all | solution.py:49
  85.1 2.7 %reduce.1 = bf16[128,1664]{1,0:T(8,128)(2,1)S(1)} reduce(bf16[128,1,1664]{2,1,0:T(2,128)(2,1)S(1)} %reshape.70, bf16[]{:T(256)} %constant.7), dimensions={1}, to_apply=%all_to_all.73.reduce_sub_computation | reduce | bytes 851970 | tf_op jit(solution)/shard_map/all_to_all | solution.py:49
  88.6 20.5 %all_to_all.86 = bf16[4,32,1664]{2,0,1:T(4,128)(2,1)S(1)} all-to-all(bf16[4,32,1664]{2,0,1:T(4,128)(2,1)S(1)} %copy.38), channel_id=1, replica_groups=mesh['dp'=8,'tensor'=32] {'tensor'}, dimensions={1} | all-to-all | bytes 851968 | tf_op jit(solution)/shard_map/all_to_all | solution.py:56
  109.1 0.9 reshape.56
  110.0 1.1 reduce-scatter.4.cloned.1.call-done
  111.1 1.3 copy.44
  112.4 1.0 reduce.2
  113.6 1.0 reshape.67
  114.6 11.6 %all-to-all-start.1 = ((bf16[32,2,3328]{2,1,0:T(2,128)(2,1)}), bf16[32,2,3328]{2,1,0:T(2,128)(2,1)S(1)}, u32[]{:S(2)}, u32[]{:S(2)}) async-start(bf16[32,2,3328]{2,1,0:T(2,128)(2,1)} %reshape.67), calls=%async_computation.1 | async-start | bytes 851968 | tf_op jit(solution)/shard_map/all_to_all | solution.py:49
  126.3 39.0 %all-gather.2.cloned.1.call-done = bf16[1024,1664]{1,0:T(8,128)(2,1)} async-done(((bf16[128,1664]{1,0:T(8,128)(2,1)}), bf16[1024,1664]{1,0:T(8,128)(2,1)}) %all-gather.2.cloned.1.call-update) | async-done | bytes 3407888 | tf_op jit(solution)/shard_map/all_gather | solution.py:67
  165.3 5.6 %copy.39 = bf16[1664,1024]{1,0:T(8,128)(2,1)} copy(bf16[1664,1024]{0,1:T(8,128)(2,1)} %bitcast.75) | data formatting | bytes 6815744 | tf_op jit(solution)/shard_map/dot_general | solution.py:66
  171.2 3.4 %reduce = bf16[128,1664]{1,0:T(8,128)(2,1)} reduce(bf16[128,1,1664]{2,1,0:T(2,128)(2,1)S(1)} %reshape.68, bf16[]{:T(256)} %constant.7), dimensions={1}, to_apply=%all_to_all.66.reduce_sub_computation | reduce | bytes 851970 | tf_op jit(solution)/shard_map/all_to_all | solution.py:49
  174.6 2.0 all_to_all.67
  176.7 1.5 fusion.5
  178.2 1.0 copy.29
  179.1 10.5 %all-to-all-start.2 = ((bf16[4,32,1664]{2,0,1:T(4,128)(2,1)}), bf16[4,32,1664]{2,0,1:T(4,128)(2,1)}, u32[]{:S(2)}, u32[]{:S(2)}) async-start(bf16[4,32,1664]{2,0,1:T(4,128)(2,1)} %copy.29), calls=%async_computation.2 | async-start | bytes 851968 | tf_op jit(solution)/shard_map/all_to_all | solution.py:56
  189.7 9.3 %multiply_reduce_fusion = (f32[13,1024]{1,0:T(8,128)}, bf16[13,128,1024]{2,1,0:T(8,128)(2,1)}) fusion(f32[13,1024]{1,0:T(8,128)S(1)} %convert_multiply_fusion, bf16[13,128,1024]{2,1,0:T(8,128)(2,1)} %bitcast.76, bf16[1024,1024,1]{1,0,2:T(8,128)(2,1)} %bitcast.27, bf16[13,128,1024]{2,1,0:T(8,128)(2,1)S(1)} %bitcast.74), kind=kOutput, calls=%fused_computation.2 | convolution fusion | flops 3498167296 | bytes 12427264 | tf_op jit(solution)/shard_map/dot_general | solution.py:66
  199.0 5.7 %all-to-all-done.2 = bf16[4,32,1664]{2,0,1:T(4,128)(2,1)} async-done(((bf16[4,32,1664]{2,0,1:T(4,128)(2,1)}), bf16[4,32,1664]{2,0,1:T(4,128)(2,1)}, u32[]{:S(2)}, u32[]{:S(2)}) %all-to-all-start.2) | async-done | bytes 426016 | tf_op jit(solution)/shard_map/all_to_all | solution.py:56
  204.7 1.3 dot_general.34
  206.3 1.6 fusion.9
  208.4 1.0 copy.40
  (31 shorter events, 4.3 us)
Async XLA Ops:
  7.2 47.7 %copy-start = (f32[13,13]{1,0:T(8,128)S(1)}, f32[13,13]{1,0:T(8,128)}, u32[]{:S(2)}) copy-start(f32[13,13]{1,0:T(8,128)} %param.11) | copy-start | bytes 2032
  7.2 9.3 %copy-start.1 = (bf16[1664,1024]{1,0:T(8,128)(2,1)S(1)}, bf16[1664,1024]{1,0:T(8,128)(2,1)}, u32[]{:S(2)}) copy-start(bf16[1664,1024]{1,0:T(8,128)(2,1)} %param.8) | copy-start | bytes 10223620
  7.2 9.3 %copy-start.4 = (f32[13,1024]{1,0:T(8,128)S(1)}, f32[13,1024]{1,0:T(8,128)}, u32[]{:S(2)}) copy-start(f32[13,1024]{1,0:T(8,128)} %param.9) | copy-start | bytes 159748
  10.5 32.2 %all-to-all-start = ((bf16[128,8,1024]{2,0,1:T(8,128)(2,1)}), bf16[128,8,1024]{2,0,1:T(8,128)(2,1)}, u32[]{:S(2)}, u32[]{:S(2)}) async-start(bf16[128,8,1024]{2,0,1:T(8,128)(2,1)} %bitcast.73), calls=%async_computation | async-start | bytes 4194304 | tf_op jit(solution)/shard_map/all_to_all | solution.py:64
  16.5 94.6 %reduce-scatter.4.cloned.1.call-start = ((), (), s32[]{:S(2)}) async-start(), calls=%async_computation.7 | async-start | bytes 3833856
  52.6 1.0 copy-start.3
  52.6 112.7 %all-gather.2.cloned.1.call-start = ((), (), s32[]{:S(2)}) async-start(), calls=%async_computation.6 | async-start | bytes 3833856 | tf_op jit(solution)/shard_map/all_gather | solution.py:67
  88.6 37.7 %copy-start.5 = (s32[13,1024]{1,0:T(8,128)S(1)}, s32[13,1024]{1,0:T(8,128)}, u32[]{:S(2)}) copy-start(s32[13,1024]{1,0:T(8,128)} %param.10) | copy-start | bytes 159748
  114.6 56.3 %all-to-all-start.1 = ((bf16[32,2,3328]{2,1,0:T(2,128)(2,1)}), bf16[32,2,3328]{2,1,0:T(2,128)(2,1)S(1)}, u32[]{:S(2)}, u32[]{:S(2)}) async-start(bf16[32,2,3328]{2,1,0:T(2,128)(2,1)} %reshape.67), calls=%async_computation.1 | async-start | bytes 851968 | tf_op jit(solution)/shard_map/all_to_all | solution.py:49
  174.6 15.0 %copy-start.2 = (bf16[1664,1024]{1,0:T(8,128)(2,1)S(1)}, bf16[1664,1024]{1,0:T(8,128)(2,1)}, u32[]{:S(2)}) copy-start(bf16[1664,1024]{1,0:T(8,128)(2,1)} %param.8) | copy-start | bytes 10223620
  179.1 25.5 %all-to-all-start.2 = ((bf16[4,32,1664]{2,0,1:T(4,128)(2,1)}), bf16[4,32,1664]{2,0,1:T(4,128)(2,1)}, u32[]{:S(2)}, u32[]{:S(2)}) async-start(bf16[4,32,1664]{2,0,1:T(4,128)(2,1)} %copy.29), calls=%async_computation.2 | async-start | bytes 851968 | tf_op jit(solution)/shard_map/all_to_all | solution.py:56
Sparse Core Ops, SparseCore 0:
  52.7 58.3 reduce-scatter.3
  112.9 52.3 all-gather.1
where the time goes:
time: 217 us; the launch traced here: 216 us
  waiting for transfers between devices  69.3 us (32%)
  blocking collectives  46.9 us (22%)
  starting transfers between devices  28.2 us (13%)
  local copies, waits for them, and re-layouts  25.8 us (12%)
  matrix products  21 us (10%)
  between operations  14.3 us (7%)
  other arithmetic  10.8 us (5%)
    all_gather x1, waiting for transfers between devices, shards(): lax.all_gather(rotated, 'dp', axis=0, tiled=True)  39 us
    all_to_all x1, blocking collectives, cross_apply(): lax.all_to_all(values.reshape(rows, 1, width), 'tensor', split_axis=0, co...  26.4 us
    all_to_all x1, waiting for transfers between devices, shards(): lax.all_to_all(upstream, 'dp', split_axis=1, concat_axis=0, tiled=True)  23.4 us
    all_to_all x1, blocking collectives, cross_apply(): lax.all_to_all(summed, 'tensor', split_axis=1, concat_axis=0, tiled=True)  20.5 us
    all_to_all x1, starting transfers between devices, cross_apply(): lax.all_to_all(values.reshape(rows, 1, width), 'tensor', split_axis=0, co...  11.6 us
    all_to_all x1, starting transfers between devices, cross_apply(): lax.all_to_all(summed, 'tensor', split_axis=1, concat_axis=0, tiled=True)  10.5 us
    dot_general x1, matrix products, shards(): lax.dot_general(lax.all_gather(rotated, 'dp', axis=0, tiled=True), part,...  9.27 us
    unnamed x21, local copies, waits for them, and re-layouts  9.22 us
  transfers between devices with their start and end apart: 5, of which 4 were waited for; matrix products, arithmetic and copies ran while one was open for 14% of the time, Pallas kernels for 0%

commit v1 on v0

v1 whole, which is shorter than its diff:
```python
import jax
import jax.numpy as jnp
import numpy as np
from jax import lax
from jax.experimental import pallas as pl
from jax.experimental.pallas import tpu as pltpu
from jax.sharding import PartitionSpec as P

MESH = pl.DeviceIdType.MESH
BF = jnp.bfloat16
F32 = jnp.float32
HB = 128
NC = 13
W = NC * HB
E = 1024
CHUNKS = ((0, 768), (768, 1664))
N_SEM = 160


def sign_matrix(size):
    table = np.ones((1, 1), np.float32)
    while table.shape[0] < size:
        table = np.block([[table, table], [table, -table]])
    return table


def kernel(
    h_ref, up_hbm, w_hbm, sc_ref, mk_ref, rot_ref, s128_ref, k8_ref,
    gh_hbm, gw_hbm, gs_ref,
    w_v, wq, up, first, loc, loc_in, u, z_in, z_out, wz, xa, xa_send, rot, rot_t,
    part, r1, r2, t_in, comp, x_in, g, g_in, gu, gz_in, gz_out, mixed, gh_v, acc, gw_v,
    ssem, rsem, lsem,
):
    dp, tensor = lax.axis_index("dp"), lax.axis_index("tensor")
    xl, y = dp // 4, dp % 4
    z, xh, c = tensor // 4, (tensor // 2) % 2, tensor % 2
    sign_c = (1 - 2 * c).astype(F32)
    sign_x = (1 - 2 * xh).astype(F32)
    count = [0]

    def y_dev(d):
        return (xl * 4 + (y + d) % 4, tensor)

    def x_dev(q, d=0):
        return ((1 - xl) * 4 + (y + d) % 4, z * 4 + ((xh + q) % 2) * 2 + c)

    def z_dev(k):
        return (dp, ((z + k) % 8) * 4 + xh * 2 + c)

    core_dev = (dp, z * 4 + xh * 2 + (1 - c))

    def send(src, dst, dev):
        i = count[0]
        count[0] += 1
        cp = pltpu.make_async_remote_copy(
            src_ref=src, dst_ref=dst, send_sem=ssem.at[i], recv_sem=rsem.at[i],
            device_id=dev, device_id_type=MESH,
        )
        cp.start()
        sent.append(cp)
        return cp

    sent = []

    def rows(start, size, step):
        return pl.ds(pl.multiple_of(start, step), size)

    def by_cols(c0, c1, body):
        @pl.loop(c0 // HB, c1 // HB)
        def _(i):
            body(pl.ds(pl.multiple_of(i * HB, HB), HB))

    def wide(ref, *at):
        return ref[at].astype(F32)

    w_load = pltpu.make_async_copy(w_hbm, w_v, lsem.at[0])
    w_load.start()
    own_up = pltpu.make_async_copy(
        up_hbm.at[:, pl.ds(pl.multiple_of(dp * E, E), E)], up.at[pl.ds(0, HB)], lsem.at[1]
    )
    own_up.start()
    peers = [y_dev(d) for d in (1, 2, 3)] + [x_dev(q, d) for d in range(4) for q in range(2)]
    peers += [z_dev(k) for k in range(1, 8)] + [core_dev]
    barrier = pltpu.get_barrier_semaphore()
    for dev in peers:
        pl.semaphore_signal(barrier, inc=1, device_id=dev, device_id_type=MESH)
    pl.semaphore_wait(barrier, len(peers))

    up_cp = {}
    for d in (2, 1, 3, 0):
        if d:
            to = xl * 4 + (y + d) % 4
            at = rows(c * 64, 64, 64)
            up_cp[(4 - d) % 4, 0] = [
                send(
                    up_hbm.at[at, pl.ds(pl.multiple_of(to * E, E), E)],
                    up.at[rows(((4 - d) % 4) * 256 + c * 64, 64, 64)],
                    y_dev(d),
                )
            ]
        to = (1 - xl) * 4 + (y + d) % 4
        at = rows(c * 64 + xh * 32, 32, 32)
        up_cp[(4 - d) % 4, 1] = [
            send(
                up_hbm.at[at, pl.ds(pl.multiple_of(to * E, E), E)],
                up.at[rows(((4 - d) % 4) * 256 + HB + c * 64 + xh * 32, 32, 32)],
                x_dev(q, d),
            )
            for q in range(2)
        ]

    def share_up(d):
        shared = []
        for xr in range(2):
            if (d, xr) == (0, 0):
                continue
            for cp in up_cp[d, xr]:
                cp.wait_recv()
            block = up.at[rows(d * 256 + xr * HB + c * 64, 64, 64)]
            shared.append(send(block, block, core_dev))
        return shared

    def local(src, dst, coef):
        @pl.loop(0, NC)
        def _(k):
            at = pl.ds(pl.multiple_of(k * HB, HB), HB)
            first[k] = jnp.dot(src[:, at], s128_ref[...], preferred_element_type=F32)

        @pl.loop(0, 4)
        def _(i):
            at = rows(i * 32, 32, 32)
            parts = [first[k, at, :] for k in range(NC)]
            for o in range(NC):
                total = parts[0] * coef(0, o)
                for k in range(1, NC):
                    total = total + parts[k] * coef(k, o)
                dst[at, o * HB : (o + 1) * HB] = (total * HB**-0.5).astype(BF)

    local(h_ref, loc, lambda k, o: rot_ref[k, o])
    core_a = send(loc, loc_in, core_dev)

    w_load.wait()

    @pl.loop(0, NC)
    def _(i):
        at = rows(i * HB, HB, HB)
        wq[at, :] = (w_v[at, :].astype(F32) * sc_ref[pl.ds(i, 1), :]).astype(BF)

    def z_start(src, dst, cols):
        at = rows(z * 16, 16, 16)
        cps = [
            send(src.at[rows(((z + k) % 8) * 16, 16, 16), cols], dst.at[at, cols], z_dev(k))
            for k in (4, 3, 5, 2, 6, 1, 7)
        ]
        dst[at, cols] = src[at, cols]
        return cps

    def z_mix(src, dst, c0, c1):
        def body(at):
            mix = jnp.dot(k8_ref[...], src[:, at], preferred_element_type=F32)
            dst[:, at] = (mix * 32.0**-0.5).astype(BF)

        by_cols(c0, c1, body)

    def recv(cps):
        for cp in cps:
            cp.wait_recv()

    core_a.wait_recv()

    def body(at):
        u[:, at] = (wide(loc, slice(None), at) * sign_c + wide(loc_in, slice(None), at)).astype(BF)

    by_cols(0, W, body)
    za = z_start(u, z_in, slice(0, W))

    def multiply(d, c0, c1):
        def tile(at):
            r = lax.dot_general(
                up[d * 256 : (d + 1) * 256, :], wq[at, :], (((1,), (1,)), ((), ())),
                preferred_element_type=F32,
            )
            part[d, :, at] = r.astype(BF)

        @pl.loop(c0 // 256, c1 // 256)
        def _(i):
            tile(pl.ds(pl.multiple_of(i * 256, 256), 256))

        if c1 % 256:
            tile(slice(c1 - HB, c1))

    r1_cp, r2_cp = {}, {}

    def y_first(j):
        cols = slice(*CHUNKS[j])
        r1_cp[j] = [
            send(part.at[2, pl.ds(0, HB), cols], r1.at[0, :, cols], y_dev(1)),
            send(part.at[2, pl.ds(HB, HB), cols], r1.at[1, :, cols], y_dev(3)),
        ]

    def y_direct(j):
        cols = slice(*CHUNKS[j])
        r2_cp[j] = [
            send(part.at[1, pl.ds(HB, HB), cols], r2.at[0, pl.ds(HB, HB), cols], y_dev(1)),
            send(part.at[3, pl.ds(0, HB), cols], r2.at[1, pl.ds(0, HB), cols], y_dev(3)),
        ]

    def y_second(j):
        cols = slice(*CHUNKS[j])
        recv(r1_cp[j])

        def body(at):
            lo, hi = slice(0, HB), slice(HB, 256)
            part[1, lo, at] = (wide(part, 1, lo, at) + wide(r1, 0, slice(None), at)).astype(BF)
            part[3, hi, at] = (wide(part, 3, hi, at) + wide(r1, 1, slice(None), at)).astype(BF)

        by_cols(*CHUNKS[j], body)
        r2_cp[j] += [
            send(part.at[1, pl.ds(0, HB), cols], r2.at[0, pl.ds(0, HB), cols], y_dev(1)),
            send(part.at[3, pl.ds(HB, HB), cols], r2.at[1, pl.ds(HB, HB), cols], y_dev(3)),
        ]

    t_cp, x_cp, g_cp, gz_cp, gw_cp = {}, {}, {}, {}, {}

    def x_first(j):
        cols = slice(*CHUNKS[j])
        recv(r2_cp[j])

        def body(at):
            part[0, :, at] = (
                wide(part, 0, slice(None), at) + wide(r2, 0, slice(None), at) + wide(r2, 1, slice(None), at)
            ).astype(BF)

        by_cols(*CHUNKS[j], body)
        t_cp[j] = [
            send(part.at[0, rows(((xh + q) % 2) * 64, 64, 64), cols], t_in.at[q, :, cols], x_dev(q))
            for q in range(2)
        ]
        x_cp[j] = [
            send(
                part.at[0, rows(HB + (1 - xh) * 64, 64, 64), cols],
                x_in.at[q, rows((1 - xh) * 64, 64, 64), cols],
                x_dev(q),
            )
            for q in range(2)
        ]

    def x_second(j):
        cols = slice(*CHUNKS[j])
        recv(t_cp[j])

        def body(at):
            own = wide(part, 0, rows(HB + xh * 64, 64, 64), at)
            comp[0, :, at] = (own * sign_x + wide(t_in, 1, slice(None), at)).astype(BF)
            comp[1, :, at] = (own + wide(t_in, 0, slice(None), at)).astype(BF)

        by_cols(*CHUNKS[j], body)
        x_cp[j] += [
            send(comp.at[q, :, cols], x_in.at[q, rows(xh * 64, 64, 64), cols], x_dev(q)) for q in range(2)
        ]

    def core_first(j):
        cols = slice(*CHUNKS[j])
        recv(x_cp[j])

        def body(at):
            near, far = rows(xh * 64, 64, 64), rows((1 - xh) * 64, 64, 64)
            g[near, at] = (
                wide(part, 0, near, at) * sign_x + wide(x_in, 0, near, at) + wide(x_in, 1, near, at)
            ).astype(BF)
            g[far, at] = (
                (wide(part, 0, far, at) + wide(x_in, 0, far, at)) * sign_x + wide(x_in, 1, far, at)
            ).astype(BF)

        by_cols(*CHUNKS[j], body)
        g_cp[j] = send(g.at[:, cols], g_in.at[:, cols], core_dev)

    def core_second(j):
        g_cp[j].wait_recv()

        def body(at):
            gu[:, at] = (wide(g, slice(None), at) * sign_c + wide(g_in, slice(None), at)).astype(BF)

        by_cols(*CHUNKS[j], body)
        gz_cp[j] = z_start(gu, gz_in, slice(*CHUNKS[j]))

    def z_second(j):
        recv(gz_cp[j])
        z_mix(gz_in, gz_out, *CHUNKS[j])
        gw_cp[j] = z_start(gz_out, mixed, slice(*CHUNKS[j]))

    def turn(d):
        at_t = slice(d * 256, (d + 1) * 256)

        @pl.loop(0, NC)
        def _(i):
            at = rows(i * HB, HB, HB)
            rot_t[at, at_t] = rot[at_t, at].T

    def add_grad(d, at, fresh):
        own = slice(d * 256, (d + 1) * 256)
        term = jnp.dot(rot_t[:, own], up[own, at], preferred_element_type=F32)
        acc[:, at] = term if fresh else acc[:, at] + term

    def grad_step(d, fresh=False):
        turn(d)

        @pl.loop(0, 4)
        def _(i):
            add_grad(d, rows(i * 256, 256, 256), fresh)

    def rot_slot(d, xr, at=slice(None)):
        return rot.at[pl.ds(d * 256 + xr * HB, HB)]

    def rot_part(d, xr, lo):
        return rot.at[pl.ds(d * 256 + xr * HB + lo, 64)]

    def gather_first(xr):
        return {
            3: send(rot_slot(0, xr), rot_slot(3, xr), y_dev(1)),
            1: send(rot_slot(0, xr), rot_slot(1, xr), y_dev(3)),
        }

    def gather_second(cps, xr):
        cps[3].wait_recv()
        one = send(rot_part(3, xr, 0), rot_part(2, xr, 0), y_dev(1))
        cps[1].wait_recv()
        two = send(rot_part(1, xr, 64), rot_part(2, xr, 64), y_dev(3))
        return [one, two]

    shared = share_up(2)
    recv(shared)
    multiply(2, 0, W)
    y_first(0)
    shared = share_up(1) + share_up(3)
    recv(shared)
    multiply(1, 0, W)
    multiply(3, 0, W)
    y_direct(0)
    y_first(1)
    shared = share_up(0)

    recv(za)
    z_mix(z_in, z_out, 0, W)
    zb = z_start(z_out, wz, slice(0, W))

    recv(shared)
    own_up.wait()
    multiply(0, 0, W)
    y_second(0)
    y_direct(1)

    recv(zb)
    xa_cp = [send(wz, xa.at[q], x_dev(q)) for q in range(2)]
    x_first(0)
    y_second(1)
    x_second(0)
    recv(xa_cp)

    def body(at):
        a0, a1 = wide(xa, 0, slice(None), at), wide(xa, 1, slice(None), at)
        rot[HB:256, at] = (a0 * sign_x + a1).astype(BF)
        xa_send[:, at] = (a0 - a1 * sign_x).astype(BF)

    by_cols(0, W, body)
    half = rows(xh * 64, 64, 64)
    xb_cp = [
        send(rot.at[rows(HB + xh * 64, 64, 64)], rot.at[half], x_dev(0)),
        send(xa_send.at[half], rot.at[half], x_dev(1)),
    ]
    far_cp = gather_first(1)
    core_first(0)
    core_second(0)
    x_first(1)
    recv(xb_cp)
    near_cp = gather_first(0)
    x_second(1)
    z_second(0)
    grad_step(0, True)
    core_first(1)
    core_second(1)
    last = gather_second(far_cp, 1)
    z_second(1)
    last += gather_second(near_cp, 0)
    grad_step(1)
    grad_step(3)
    recv(gw_cp[0])
    recv(gw_cp[1])
    local(mixed, gh_v, lambda k, o: rot_ref[o, k])
    gh_out = pltpu.make_async_copy(gh_v, gh_hbm, lsem.at[2])
    gh_out.start()

    recv(last)
    turn(2)
    outs = []
    for i in range(4):
        at = slice(i * 256, (i + 1) * 256)
        add_grad(2, at, False)

        @pl.loop(0, NC)
        def _(k):
            group = rows(k * HB, HB, HB)
            one = pl.ds(k, 1)
            grad = acc[group, at]
            gs_ref[one, at] = jnp.sum(grad * w_v[group, at].astype(F32), axis=0, keepdims=True)
            gw_v[group, at] = (grad * (sc_ref[one, at] * mk_ref[one, at].astype(F32))).astype(BF)

        outs.append(pltpu.make_async_copy(gw_v.at[:, at], gw_hbm.at[:, at], lsem.at[3 + i]))
        outs[-1].start()
    for cp in outs:
        cp.wait()
    gh_out.wait()
    for cp in sent:
        cp.wait_send()


def solution(mesh):
    def step(hidden, upstream, weight, scales, clip_mask, rot_block):
        s128 = jnp.asarray(sign_matrix(HB), BF)
        k8 = jnp.asarray(np.kron(sign_matrix(8), np.eye(16, dtype=np.float32)), BF)
        vmem = pl.BlockSpec(memory_space=pltpu.VMEM)
        smem = pl.BlockSpec(memory_space=pltpu.SMEM)
        anywhere = pl.BlockSpec(memory_space=pl.ANY)
        full = pltpu.VMEM((HB, W), BF)
        two = pltpu.VMEM((2, HB, W), BF)
        tall = pltpu.VMEM((8 * HB, W), BF)
        wide = pltpu.VMEM((W, E), BF)
        scratch = [
            wide, wide, pltpu.VMEM((8 * HB, E), BF), pltpu.VMEM((NC, HB, HB), F32),
            full, full, full, full, full, full, two, full, tall, wide,
            pltpu.VMEM((4, 2 * HB, W), BF), two, pltpu.VMEM((2, 2 * HB, W), BF),
            pltpu.VMEM((2, 64, W), BF), pltpu.VMEM((2, 64, W), BF), two,
            full, full, full, full, full, full, full, pltpu.VMEM((W, E), F32), wide,
            pltpu.SemaphoreType.DMA((N_SEM,)), pltpu.SemaphoreType.DMA((N_SEM,)), pltpu.SemaphoreType.DMA((8,)),
        ]
        return pl.pallas_call(
            kernel,
            name="fused",
            out_shape=(
                jax.ShapeDtypeStruct((HB, W), BF),
                jax.ShapeDtypeStruct((W, E), BF),
                jax.ShapeDtypeStruct((NC, E), F32),
            ),
            in_specs=[vmem, anywhere, anywhere, vmem, vmem, smem, vmem, vmem],
            out_specs=(anywhere, anywhere, vmem),
            scratch_shapes=scratch,
            compiler_params=pltpu.CompilerParams(
                collective_id=0, has_side_effects=True, vmem_limit_bytes=56 * 2**20
            ),
        )(hidden, upstream, weight, scales, clip_mask, rot_block, s128, k8)

    return jax.shard_map(
        step,
        mesh=mesh,
        in_specs=(
            P("dp", "tensor"),
            P("dp", None),
            P("tensor", "dp"),
            P("tensor", "dp"),
            P("tensor", "dp"),
            P(),
        ),
        out_specs=(P("dp", "tensor"), P("tensor", "dp"), P("tensor", "dp")),
        check_vma=False,
    )
```

time: 217 us -> 112 us (0.52)
  Pallas kernels: 0 us -> 104 us
  waiting for transfers between devices: 69.3 us -> 0 us
  blocking collectives: 46.9 us -> 0 us
  starting transfers between devices: 28.2 us -> 0 us
  matrix products: 21 us -> 0 us
  local copies, waits for them, and re-layouts: 25.8 us -> 6.51 us
  between operations: 14.3 us -> 0.64 us
  other arithmetic: 10.8 us -> 0 us
    pallas_call x0 -> x1, Pallas kernels: none -> 104 us  [step(): pl.pallas_call(kernel, name='fused', out_shape=(jax.ShapeDtypeStruct((HB,...]
    all_to_all x2 -> x0, blocking collectives: 46.9 us -> none  [the longest x1 26.4 us: cross_apply(): lax.all_to_all(values.reshape(rows, 1, width), 'tensor', split_axis=0, co...]
    all_gather x1 -> x0, waiting for transfers between devices: 39 us -> none  [shards(): lax.all_gather(rotated, 'dp', axis=0, tiled=True)]
    all_to_all x3 -> x0, waiting for transfers between devices: 29.1 us -> none  [the longest x1 23.4 us: shards(): lax.all_to_all(upstream, 'dp', split_axis=1, concat_axis=0, tiled=True)]
    all_to_all x3 -> x0, starting transfers between devices: 28.1 us -> none  [the longest x1 11.6 us: cross_apply(): lax.all_to_all(values.reshape(rows, 1, width), 'tensor', split_axis=0, co...]
    dot_general x8 -> x0, matrix products: 21 us -> none  [the longest x1 9.27 us: shards(): lax.dot_general(lax.all_gather(rotated, 'dp', axis=0, tiled=True), part,...]
    dot_general x3 -> x0, local copies, waits for them, and re-layouts: 7.15 us -> none  [the longest x1 5.57 us: shards(): lax.dot_general(lax.all_gather(rotated, 'dp', axis=0, tiled=True), part,...]
    all_to_all x2 -> x0, other arithmetic: 6.09 us -> none  [cross_apply(): lax.all_to_all(values.reshape(rows, 1, width), 'tensor', split_axis=0, co...]
  transfers between devices with their start and end apart: 5 -> 0, of which waited for: 4 -> 0; matrix products, arithmetic and copies ran while one was open for 14% -> 0% of each run, Pallas kernels for 0% -> 0%
where the time goes in v1:
time: 112 us
  Pallas kernels  104 us (93%)
  local copies, waits for them, and re-layouts  6.51 us (6%)
    pallas_call x1, Pallas kernels, step(): pl.pallas_call(kernel, name='fused', out_shape=(jax.ShapeDtypeStruct((HB,...  104 us
    unnamed x5, local copies, waits for them, and re-layouts  6.51 us

profile of v1, /device:TPU:1, one launch (start us, length us, event | category | flops | bytes accessed | tf_op | source)
XLA Modules:
  0.0 111.6 jit_solution(18277866935898775963)
XLA Ops:
  0.6 104.5 %fused.1 = (bf16[128,1664]{1,0:T(8,128)(2,1)}, bf16[1664,1024]{1,0:T(8,128)(2,1)}, f32[13,1024]{1,0:T(8,128)}) custom-call(bf16[128,1664]{1,0:T(8,128)(2,1)} %h_ref.1, bf16[128,8192]{1,0:T(8,128)(2,1)} %up_hbm.1, bf16[1664,1024]{1,0:T(8,128)(2,1)} %w_hbm.1, f32[13,1024]{1,0:T(8,128)} %sc_ref.1, s32[13,1024]{1,0:T(8,128)} %mk_ref.1, f32[13,13]{1,0:T(8,128)} %rot_ref.1, ...), custom_call_target="tpu_custom_call" | custom-call | tf_op jit(solution)/shard_map/fused/pallas_call | solution.py:436
  105.1 1.8 %copy.14 = bf16[128,1664]{1,0:T(8,128)(2,1)} copy(bf16[128,1664]{1,0:T(8,128)(2,1)} %get-tuple-element.6) | data formatting | bytes 851968
  106.9 0.0 copy-start
  106.9 4.1 %copy.15 = bf16[1664,1024]{1,0:T(8,128)(2,1)} copy(bf16[1664,1024]{1,0:T(8,128)(2,1)} %get-tuple-element.7) | data formatting | bytes 6815744
  111.0 0.0 copy-done
  111.0 0.6 copy.16
Async XLA Ops:
  106.9 4.1 %copy-start = (f32[13,1024]{1,0:T(8,128)S(1)}, f32[13,1024]{1,0:T(8,128)}, u32[]{:S(2)}) copy-start(f32[13,1024]{1,0:T(8,128)} %get-tuple-element.8) | copy-start | bytes 159748

commit v2 on v0

v2 whole, which is shorter than its diff:
```python
import jax
import jax.numpy as jnp
import numpy as np
from jax import lax
from jax.experimental import pallas as pl
from jax.experimental.pallas import tpu as pltpu
from jax.sharding import PartitionSpec as P

MESH = pl.DeviceIdType.MESH
BF = jnp.bfloat16
F32 = jnp.float32
HB = 128
NC = 13
W = NC * HB
E = 1024
CHUNKS = ((0, 768), (768, 1664))
OUT_ROWS = ((0, 896), (896, 1664))
PLACE = {0: 0, 1: 256, 3: 512, 2: 768}
N_SEM = 40


def sign_matrix(size):
    table = np.ones((1, 1), np.float32)
    while table.shape[0] < size:
        table = np.block([[table, table], [table, -table]])
    return table


def kernel(
    h_ref, up_hbm, w_hbm, sc_ref, mk_ref, rot_ref, s128_ref,
    gh_hbm, gw_hbm, gs_hbm,
    up_v, w_v, wq, up, first, loc, loc_in, u, z_in, z_out, wz, xa, xa_send, rot,
    part, r1, r2, t_in, comp, x_in, g, g_in, gu, gz_in, gz_out, mixed, gh_v, acc, gw_v, gs_ref,
    ssem, rsem, lsem,
):
    dp, tensor = lax.axis_index("dp"), lax.axis_index("tensor")
    xl, y = dp // 4, dp % 4
    z, xh, c = tensor // 4, (tensor // 2) % 2, tensor % 2
    sign_c = (1 - 2 * c).astype(F32)
    sign_x = (1 - 2 * xh).astype(F32)
    sent = []

    def y_dev(d):
        return (xl * 4 + (y + d) % 4, tensor)

    def x_dev(q, d=0):
        return ((1 - xl) * 4 + (y + d) % 4, z * 4 + ((xh + q) % 2) * 2 + c)

    def z_dev(k):
        return (dp, ((z + k) % 8) * 4 + xh * 2 + c)

    core_dev = (dp, z * 4 + xh * 2 + (1 - c))

    class Group:
        def __init__(self, like):
            self.like, self.i = like, len(sent)
            sent.append(self)

        def send(self, src, dst, dev):
            pltpu.make_async_remote_copy(
                src_ref=src, dst_ref=dst, send_sem=ssem.at[self.i], recv_sem=rsem.at[self.i],
                device_id=dev, device_id_type=MESH,
            ).start()
            return self

        def recv(self):
            pltpu.make_async_copy(self.like, self.like, rsem.at[self.i]).wait()

        def finish(self):
            pltpu.make_async_copy(self.like, self.like, ssem.at[self.i]).wait()

    def send(src, dst, dev):
        return Group(src).send(src, dst, dev)

    def rows(start, size, step):
        return pl.ds(pl.multiple_of(start, step), size)

    def wide(ref, *at):
        return ref[at].astype(F32)

    up_load = pltpu.make_async_copy(up_hbm, up_v, lsem.at[1])
    up_load.start()
    w_load = pltpu.make_async_copy(w_hbm, w_v, lsem.at[0])
    w_load.start()
    peers = [y_dev(d) for d in (1, 2, 3)] + [x_dev(q, d) for d in range(4) for q in range(2)]
    peers += [z_dev(k) for k in range(1, 8)] + [core_dev]
    barrier = pltpu.get_barrier_semaphore()
    for dev in peers:
        pl.semaphore_signal(barrier, inc=1, device_id=dev, device_id_type=MESH)

    def mix_blocks(store, coef):
        @pl.loop(0, 4)
        def _(i):
            at = rows(i * 32, 32, 32)
            parts = [first[k, at, :] for k in range(NC)]
            for o in range(NC):
                total = parts[0] * coef(0, o)
                for k in range(1, NC):
                    total = total + parts[k] * coef(k, o)
                store(i, o, (total * HB**-0.5).astype(BF))

    for k in range(NC):
        first[k] = lax.dot_general(
            s128_ref[...], h_ref[:, k * HB : (k + 1) * HB], (((1,), (1,)), ((), ())),
            preferred_element_type=F32,
        )

    def store_loc(i, o, value):
        loc[rows(o * HB + i * 32, 32, 32), :] = value

    mix_blocks(store_loc, lambda k, o: rot_ref[k, o])
    up_load.wait()
    pl.semaphore_wait(barrier, len(peers))

    up_cp = {}
    for d in (2, 1, 3, 0):
        slot_of = (4 - d) % 4
        there = PLACE[slot_of]
        up_cp[slot_of] = Group(up.at[pl.ds(there, HB if d else 64)])
        if d:
            to = xl * 4 + (y + d) % 4
            up_cp[slot_of].send(
                up_v.at[rows(c * 64, 64, 64), pl.ds(pl.multiple_of(to * E, E), E)],
                up.at[rows(there + c * 64, 64, 64)],
                y_dev(d),
            )
        to = (1 - xl) * 4 + (y + d) % 4
        quarter = c * 64 + xh * 32
        for q in range(2):
            up_cp[slot_of].send(
                up_v.at[rows(quarter, 32, 32), pl.ds(pl.multiple_of(to * E, E), E)],
                up.at[rows(there + HB + quarter, 32, 32)],
                x_dev(q, d),
            )
    core_a = send(loc, loc_in, core_dev)

    def share_up(d):
        up_cp[d].recv()
        shared = Group(up.at[pl.ds(PLACE[d], HB if d else 64)])
        for xr in range(0 if d else 1, 2):
            block = up.at[rows(PLACE[d] + xr * HB + c * 64, 64, 64)]
            shared.send(block, block, core_dev)
        return shared

    w_load.wait()

    @pl.loop(0, NC)
    def _(i):
        at = rows(i * HB, HB, HB)
        wq[at, :] = (w_v[at, :].astype(F32) * sc_ref[pl.ds(i, 1), :]).astype(BF)

    def z_start(src, dst, r0, r1_):
        b = (r1_ - r0) // 8
        at = rows(r0 + z * b, b, 16)
        group = Group(dst.at[pl.ds(r0, 7 * b)])
        for k in (4, 3, 5, 2, 6, 1, 7):
            group.send(src.at[rows(r0 + ((z + k) % 8) * b, b, 16)], dst.at[at], z_dev(k))
        dst[at, :] = src[at, :]
        return group

    def z_mix(src, dst, r0, r1_):
        b = (r1_ - r0) // 8

        @pl.loop(0, b // 16)
        def _(i):
            at = [rows(r0 + k * b + i * 16, 16, 16) for k in range(8)]
            v = [wide(src, at[k]) for k in range(8)]
            for bit in (1, 2, 4):
                v = [v[k ^ bit] - v[k] if k & bit else v[k] + v[k | bit] for k in range(8)]
            for k in range(8):
                dst[at[k], :] = (v[k] * 32.0**-0.5).astype(BF)

    core_a.recv()
    u[...] = (wide(loc, ...) * sign_c + wide(loc_in, ...)).astype(BF)
    za = [z_start(u, z_in, *rs) for rs in CHUNKS]

    def multiply(d):
        group = up[PLACE[d] : PLACE[d] + 256, :]
        r = lax.dot_general(wq[...], group, (((1,), (1,)), ((), ())), preferred_element_type=F32)
        for xr in range(2):
            part[d, xr] = r[:, xr * HB : (xr + 1) * HB].astype(BF)

    r1_cp, r2_cp = {}, {}

    def chunk(j):
        return pl.ds(CHUNKS[j][0], CHUNKS[j][1] - CHUNKS[j][0])

    def y_first(j):
        at = chunk(j)
        r1_cp[j] = [
            send(part.at[2, 0, at], r1.at[0, at], y_dev(1)),
            send(part.at[2, 1, at], r1.at[1, at], y_dev(3)),
        ]

    def y_direct(j):
        at = chunk(j)
        r2_cp[j] = Group(r2.at[:, :, at])
        r2_cp[j].send(part.at[1, 1, at], r2.at[0, 1, at], y_dev(1))
        r2_cp[j].send(part.at[3, 0, at], r2.at[1, 0, at], y_dev(3))

    def y_second(j):
        at = chunk(j)
        r1_cp[j][0].recv()
        part[1, 0, at] = (wide(part, 1, 0, at) + wide(r1, 0, at)).astype(BF)
        r2_cp[j].send(part.at[1, 0, at], r2.at[0, 0, at], y_dev(1))
        r1_cp[j][1].recv()
        part[3, 1, at] = (wide(part, 3, 1, at) + wide(r1, 1, at)).astype(BF)
        r2_cp[j].send(part.at[3, 1, at], r2.at[1, 1, at], y_dev(3))

    t_cp, x_cp, g_cp, gz_cp, gw_cp = {}, {}, {}, {}, {}

    def half(j, which):
        r0, r1_ = CHUNKS[j]
        return rows(r0 + which * ((r1_ - r0) // 2), (r1_ - r0) // 2, 64)

    def packed(j):
        r0, r1_ = CHUNKS[j]
        return pl.ds(r0 // 2, (r1_ - r0) // 2)

    def x_first(j):
        at = chunk(j)
        r2_cp[j].recv()
        for xr in range(2):
            total = wide(part, 0, xr, at) + wide(r2, 0, xr, at) + wide(r2, 1, xr, at)
            part[0, xr, at] = total.astype(BF)
        t_cp[j], x_cp[j] = Group(t_in.at[:, packed(j)]), Group(x_in.at[:, at])
        other = half(j, 1 - xh)
        for q in range(2):
            t_cp[j].send(part.at[0, 0, half(j, (xh + q) % 2)], t_in.at[q, packed(j)], x_dev(q))
        for q in range(2):
            x_cp[j].send(part.at[0, 1, other], x_in.at[q, other], x_dev(q))

    def x_second(j):
        mine, there = half(j, xh), packed(j)
        t_cp[j].recv()
        own = wide(part, 0, 1, mine)
        comp[0, there] = (own * sign_x + wide(t_in, 1, there)).astype(BF)
        comp[1, there] = (own + wide(t_in, 0, there)).astype(BF)
        for q in range(2):
            x_cp[j].send(comp.at[q, there], x_in.at[q, mine], x_dev(q))

    def core_first(j):
        x_cp[j].recv()
        near, far = half(j, xh), half(j, 1 - xh)
        g[near, :] = (wide(part, 0, 0, near) * sign_x + wide(x_in, 0, near) + wide(x_in, 1, near)).astype(BF)
        g[far, :] = ((wide(part, 0, 0, far) + wide(x_in, 0, far)) * sign_x + wide(x_in, 1, far)).astype(BF)
        g_cp[j] = send(g.at[chunk(j)], g_in.at[chunk(j)], core_dev)

    def core_second(j):
        at = chunk(j)
        g_cp[j].recv()
        gu[at, :] = (wide(g, at) * sign_c + wide(g_in, at)).astype(BF)
        gz_cp[j] = z_start(gu, gz_in, *CHUNKS[j])

    def z_second(j):
        gz_cp[j].recv()
        z_mix(gz_in, gz_out, *CHUNKS[j])
        gw_cp[j] = z_start(gz_out, mixed, *CHUNKS[j])

    def add_grad(slots, r0, r1_, fresh):
        tokens = slice(slots[0] * HB, (slots[-1] + 1) * HB)

        @pl.loop(0, 2)
        def _(i):
            columns = rows(i * 512, 512, 512)
            block = jnp.concatenate([rot[k, r0:r1_, :] for k in slots], axis=1)
            term = jnp.dot(block, up[tokens, columns], preferred_element_type=F32)
            acc[r0:r1_, columns] = term if fresh else acc[r0:r1_, columns] + term

    def grad_step(slots, fresh=False):
        for r0, r1_ in OUT_ROWS:
            add_grad(slots, r0, r1_, fresh)

    def slot(d, xr):
        return PLACE[d] // HB + xr

    def gather_first(xr):
        own = rot.at[slot(0, xr)]
        return send(own, rot.at[slot(3, xr)], y_dev(1)), send(own, rot.at[slot(1, xr)], y_dev(3))

    def gather_second(cps, xr):
        top, low = pl.ds(0, W // 2), pl.ds(W // 2, W // 2)
        cps[0].recv()
        one = send(rot.at[slot(3, xr), top], rot.at[slot(2, xr), top], y_dev(1))
        cps[1].recv()
        two = send(rot.at[slot(1, xr), low], rot.at[slot(2, xr), low], y_dev(3))
        return [one, two]

    zb = []
    def zret(j):
        za[j].recv()
        z_mix(z_in, z_out, *(CHUNKS[j] if len(za) == 2 else (0, W)))
        zb.append(z_start(z_out, wz, *(CHUNKS[j] if len(za) == 2 else (0, W))))
    xa_cp = Group(xa)
    def xa_start(j):
        zb[j].recv()
        at = chunk(j) if len(za) == 2 else pl.ds(0, W)
        for q in range(2):
            xa_cp.send(wz.at[at], xa.at[q, at], x_dev(q))
    def p0():
        shared.recv()
        up[0:HB, :] = up_v[:, pl.ds(pl.multiple_of(dp * E, E), E)]
        multiply(0)
    def xmid():
        xa_cp.recv()
        rot[slot(0, 1)] = (wide(xa, 0) * sign_x + wide(xa, 1)).astype(BF)
        xa_send[...] = (wide(xa, 0) - wide(xa, 1) * sign_x).astype(BF)
        own_half = rows(xh * (W // 2), W // 2, W // 2)
        xb_cp = Group(rot.at[slot(0, 0)])
        xb_cp.send(rot.at[slot(0, 1), own_half], rot.at[slot(0, 0), own_half], x_dev(0))
        xb_cp.send(xa_send.at[own_half], rot.at[slot(0, 0), own_half], x_dev(1))
        return xb_cp
    shared = share_up(2)
    shared.recv()
    multiply(2)
    y_first(0)
    shared = share_up(1), share_up(3)
    shared[0].recv()
    shared[1].recv()
    multiply(1)
    multiply(3)
    y_direct(0)
    y_first(1)
    shared = share_up(0)
    for j in range(len(za)): zret(j)
    p0()
    y_second(0)
    y_direct(1)
    for j in range(len(za)): xa_start(j)
    x_first(0)
    y_second(1)
    x_second(0)
    xb_cp = xmid()
    far_cp = gather_first(1)
    core_first(0)
    core_second(0)
    x_first(1)
    xb_cp.recv()
    near_cp = gather_first(0)
    x_second(1)
    z_second(0)
    grad_step((0, 1), True)
    core_first(1)
    core_second(1)
    last = gather_second(far_cp, 1)
    z_second(1)
    last += gather_second(near_cp, 0)
    grad_step((2, 3, 4, 5))
    gw_cp[0].recv()
    gw_cp[1].recv()
    for k in range(NC):
        first[k] = lax.dot_general(
            mixed[k * HB : (k + 1) * HB, :], s128_ref[...], (((0,), (0,)), ((), ())),
            preferred_element_type=F32,
        )

    def store_gh(i, o, value):
        gh_v[rows(i * 32, 32, 32), o * HB : (o + 1) * HB] = value

    mix_blocks(store_gh, lambda k, o: rot_ref[o, k])
    gh_out = pltpu.make_async_copy(gh_v, gh_hbm, lsem.at[2])
    gh_out.start()

    for cp in last:
        cp.recv()
    outs = []
    for i, (r0, r1_) in enumerate(OUT_ROWS):
        add_grad((6, 7), r0, r1_, False)

        @pl.loop(r0 // HB, r1_ // HB)
        def _(k):
            group = rows(k * HB, HB, HB)
            one = pl.ds(k, 1)
            for at in (slice(0, 512), slice(512, 1024)):
                grad = acc[group, at]
                gs_ref[one, at] = jnp.sum(grad * w_v[group, at].astype(F32), axis=0, keepdims=True)
                gw_v[group, at] = (grad * (sc_ref[one, at] * mk_ref[one, at].astype(F32))).astype(BF)

        done = pl.ds(r0, r1_ - r0)
        outs.append(pltpu.make_async_copy(gw_v.at[done], gw_hbm.at[done], lsem.at[3 + i]))
        outs[-1].start()
    outs.append(pltpu.make_async_copy(gs_ref, gs_hbm, lsem.at[5]))
    outs[-1].start()
    for cp in outs:
        cp.wait()
    gh_out.wait()
    for group in sent:
        group.finish()


def hand_over(gh, gw, gs, gh_out, gw_out, gs_out, gh_v, gw_v, gs_v, sem):
    pieces = [(gw.at[at], gw_v.at[at], gw_out.at[at]) for at in (pl.ds(i * 208, 208) for i in range(8))]
    pieces += [(gh, gh_v, gh_out), (gs, gs_v, gs_out)]
    into = [pltpu.make_async_copy(a, b, sem.at[0, i]) for i, (a, b, _) in enumerate(pieces)]
    out = [pltpu.make_async_copy(b, c, sem.at[1, i]) for i, (_, b, c) in enumerate(pieces)]
    for cp in into:
        cp.start()
    for first, then in zip(into, out):
        first.wait()
        then.start()
    for cp in out:
        cp.wait()


def solution(mesh):
    def step(hidden, upstream, weight, scales, clip_mask, rot_block):
        s128 = jnp.asarray(sign_matrix(HB), BF)
        vmem = pl.BlockSpec(memory_space=pltpu.VMEM)
        smem = pl.BlockSpec(memory_space=pltpu.SMEM)
        anywhere = pl.BlockSpec(memory_space=pl.ANY)
        full = pltpu.VMEM((W, HB), BF)
        two = pltpu.VMEM((2, W, HB), BF)
        halves = pltpu.VMEM((2, W // 2, HB), BF)
        whole = pltpu.VMEM((W, E), BF)
        scratch = [
            pltpu.VMEM((HB, 8 * E), BF), whole, whole, pltpu.VMEM((8 * HB, E), BF), pltpu.VMEM((NC, HB, HB), F32),
            full, full, full, full, full, full, two, full, pltpu.VMEM((8, W, HB), BF),
            pltpu.VMEM((4, 2, W, HB), BF), two, pltpu.VMEM((2, 2, W, HB), BF), halves, halves, two,
            full, full, full, full, full, full, pltpu.VMEM((HB, W), BF), pltpu.VMEM((W, E), F32), whole,
            pltpu.VMEM((NC, E), F32), pltpu.SemaphoreType.DMA((N_SEM,)), pltpu.SemaphoreType.DMA((N_SEM,)), pltpu.SemaphoreType.DMA((8,)),
        ]
        shapes = (
            jax.ShapeDtypeStruct((HB, W), BF),
            jax.ShapeDtypeStruct((W, E), BF),
            jax.ShapeDtypeStruct((NC, E), F32),
        )
        results = pl.pallas_call(
            kernel,
            name="fused",
            out_shape=shapes,
            in_specs=[vmem, anywhere, anywhere, vmem, vmem, smem, vmem],
            out_specs=(anywhere,) * 3,
            scratch_shapes=scratch,
            compiler_params=pltpu.CompilerParams(
                collective_id=0, has_side_effects=True, vmem_limit_bytes=56 * 2**20
            ),
        )(hidden, upstream, weight, scales, clip_mask, rot_block, s128)
        return pl.pallas_call(
            hand_over,
            name="hand_over",
            out_shape=shapes,
            in_specs=[anywhere] * 3,
            out_specs=(anywhere,) * 3,
            scratch_shapes=[
                pltpu.VMEM((HB, W), BF), whole, pltpu.VMEM((NC, E), F32), pltpu.SemaphoreType.DMA((2, 10)),
            ],
        )(*results)

    return jax.shard_map(
        step,
        mesh=mesh,
        in_specs=(
            P("dp", "tensor"),
            P("dp", None),
            P("tensor", "dp"),
            P("tensor", "dp"),
            P("tensor", "dp"),
            P(),
        ),
        out_specs=(P("dp", "tensor"), P("tensor", "dp"), P("tensor", "dp")),
        check_vma=False,
    )
```

time: 217 us -> 91.9 us (0.42)
  Pallas kernels: 0 us -> 91 us
  waiting for transfers between devices: 69.3 us -> 0 us
  blocking collectives: 46.9 us -> 0 us
  starting transfers between devices: 28.2 us -> 0 us
  local copies, waits for them, and re-layouts: 25.8 us -> 0 us
  matrix products: 21 us -> 0 us
  between operations: 14.3 us -> 0.64 us
  other arithmetic: 10.8 us -> 0 us
    pallas_call x0 -> x2, Pallas kernels: none -> 91 us  [the longest x1 87.7 us: step(): pl.pallas_call(kernel, name='fused', out_shape=shapes, in_specs=[vmem, an...]
    all_to_all x2 -> x0, blocking collectives: 46.9 us -> none  [the longest x1 26.4 us: cross_apply(): lax.all_to_all(values.reshape(rows, 1, width), 'tensor', split_axis=0, co...]
    all_gather x1 -> x0, waiting for transfers between devices: 39 us -> none  [shards(): lax.all_gather(rotated, 'dp', axis=0, tiled=True)]
    all_to_all x3 -> x0, waiting for transfers between devices: 29.1 us -> none  [the longest x1 23.4 us: shards(): lax.all_to_all(upstream, 'dp', split_axis=1, concat_axis=0, tiled=True)]
    all_to_all x3 -> x0, starting transfers between devices: 28.1 us -> none  [the longest x1 11.6 us: cross_apply(): lax.all_to_all(values.reshape(rows, 1, width), 'tensor', split_axis=0, co...]
    dot_general x8 -> x0, matrix products: 21 us -> none  [the longest x1 9.27 us: shards(): lax.dot_general(lax.all_gather(rotated, 'dp', axis=0, tiled=True), part,...]
    unnamed x21 -> x0, local copies, waits for them, and re-layouts: 9.22 us -> none
    dot_general x3 -> x0, local copies, waits for them, and re-layouts: 7.15 us -> none  [the longest x1 5.57 us: shards(): lax.dot_general(lax.all_gather(rotated, 'dp', axis=0, tiled=True), part,...]
  transfers between devices with their start and end apart: 5 -> 0, of which waited for: 4 -> 0; matrix products, arithmetic and copies ran while one was open for 14% -> 0% of each run, Pallas kernels for 0% -> 0%
where the time goes in v2:
time: 91.9 us; the launch traced here: 91.6 us
  Pallas kernels  91 us (99%)
    pallas_call x1, Pallas kernels, step(): pl.pallas_call(kernel, name='fused', out_shape=shapes, in_specs=[vmem, an...  87.7 us
    pallas_call x1, Pallas kernels, step(): pl.pallas_call(hand_over, name='hand_over', out_shape=shapes, in_specs=[a...  3.31 us

profile of v2, /device:TPU:1, one launch (start us, length us, event | category | flops | bytes accessed | tf_op | source)
XLA Modules:
  0.0 91.6 jit_solution(5506567505913031590)
XLA Ops:
  0.6 87.7 %fused.1 = (bf16[128,1664]{1,0:T(8,128)(2,1)}, bf16[1664,1024]{1,0:T(8,128)(2,1)}, f32[13,1024]{1,0:T(8,128)}) custom-call(bf16[128,1664]{1,0:T(8,128)(2,1)} %h_ref.1, bf16[128,8192]{1,0:T(8,128)(2,1)} %up_hbm.1, bf16[1664,1024]{1,0:T(8,128)(2,1)} %w_hbm.1, f32[13,1024]{1,0:T(8,128)} %sc_ref.1, s32[13,1024]{1,0:T(8,128)} %mk_ref.1, f32[13,13]{1,0:T(8,128)} %rot_ref.1, ...), custom_call_target="tpu_custom_call" | custom-call | tf_op jit(solution)/shard_map/fused/pallas_call | solution.py:427
  88.3 3.3 %hand_over.1 = (bf16[128,1664]{1,0:T(8,128)(2,1)}, bf16[1664,1024]{1,0:T(8,128)(2,1)}, f32[13,1024]{1,0:T(8,128)}) custom-call(bf16[128,1664]{1,0:T(8,128)(2,1)} %get-tuple-element.6.gh, bf16[1664,1024]{1,0:T(8,128)(2,1)} %get-tuple-element.7.gw, f32[13,1024]{1,0:T(8,128)} %get-tuple-element.8.gs), custom_call_target="tpu_custom_call" | custom-call | tf_op jit(solution)/shard_map/hand_over/pallas_call | solution.py:438

commit v3 on v2

--- a/solution.py
+++ b/solution.py
@@ -26,11 +26,27 @@
     return table
 
 
+def rows(start, size, step):
+    return pl.ds(pl.multiple_of(start, step), size)
+
+
+def mix_blocks(first, store, coef):
+    @pl.loop(0, 4)
+    def _(i):
+        at = rows(i * 32, 32, 32)
+        parts = [first[k, at, :] for k in range(NC)]
+        for o in range(NC):
+            total = parts[0] * coef(0, o)
+            for k in range(1, NC):
+                total = total + parts[k] * coef(k, o)
+            store(i, o, (total * HB**-0.5).astype(BF))
+
+
 def kernel(
-    h_ref, up_hbm, w_hbm, sc_ref, mk_ref, rot_ref, s128_ref,
-    gh_hbm, gw_hbm, gs_hbm,
+    h_ref, up_hbm, w_hbm, sc_ref, rot_ref, s128_ref,
+    mixed_hbm, last_hbm, acc_hbm, up_out,
     up_v, w_v, wq, up, first, loc, loc_in, u, z_in, z_out, wz, xa, xa_send, rot,
-    part, r1, r2, t_in, comp, x_in, g, g_in, gu, gz_in, gz_out, mixed, gh_v, acc, gw_v, gs_ref,
+    part, r1, r2, t_in, comp, x_in, g, g_in, gu, gz_in, gz_out, acc, acc_out,
     ssem, rsem, lsem,
 ):
     dp, tensor = lax.axis_index("dp"), lax.axis_index("tensor")
@@ -51,6 +67,12 @@
 
     core_dev = (dp, z * 4 + xh * 2 + (1 - c))
 
+    stores = []
+
+    def store(src, dst):
+        stores.append(pltpu.make_async_copy(src, dst, lsem.at[2 + len(stores)]))
+        stores[-1].start()
+
     class Group:
         def __init__(self, like):
             self.like, self.i = like, len(sent)
@@ -71,9 +93,6 @@
 
     def send(src, dst, dev):
         return Group(src).send(src, dst, dev)
-
-    def rows(start, size, step):
-        return pl.ds(pl.multiple_of(start, step), size)
 
     def wide(ref, *at):
         return ref[at].astype(F32)
@@ -88,17 +107,6 @@
     for dev in peers:
         pl.semaphore_signal(barrier, inc=1, device_id=dev, device_id_type=MESH)
 
-    def mix_blocks(store, coef):
-        @pl.loop(0, 4)
-        def _(i):
-            at = rows(i * 32, 32, 32)
-            parts = [first[k, at, :] for k in range(NC)]
-            for o in range(NC):
-                total = parts[0] * coef(0, o)
-                for k in range(1, NC):
-                    total = total + parts[k] * coef(k, o)
-                store(i, o, (total * HB**-0.5).astype(BF))
-
     for k in range(NC):
         first[k] = lax.dot_general(
             s128_ref[...], h_ref[:, k * HB : (k + 1) * HB], (((1,), (1,)), ((), ())),
@@ -108,12 +116,12 @@
     def store_loc(i, o, value):
         loc[rows(o * HB + i * 32, 32, 32), :] = value
 
-    mix_blocks(store_loc, lambda k, o: rot_ref[k, o])
+    mix_blocks(first, store_loc, lambda k, o: rot_ref[k, o])
     up_load.wait()
     pl.semaphore_wait(barrier, len(peers))
 
     up_cp = {}
-    for d in (2, 1, 3, 0):
+    def up_start(d):
         slot_of = (4 - d) % 4
         there = PLACE[slot_of]
         up_cp[slot_of] = Group(up.at[pl.ds(there, HB if d else 64)])
@@ -132,6 +140,8 @@
                 up.at[rows(there + HB + quarter, 32, 32)],
                 x_dev(q, d),
             )
+    up_start(2)
+    up_start(0)
     core_a = send(loc, loc_in, core_dev)
 
     def share_up(d):
@@ -155,7 +165,10 @@
         group = Group(dst.at[pl.ds(r0, 7 * b)])
         for k in (4, 3, 5, 2, 6, 1, 7):
             group.send(src.at[rows(r0 + ((z + k) % 8) * b, b, 16)], dst.at[at], z_dev(k))
-        dst[at, :] = src[at, :]
+        if dst is mixed_hbm:
+            store(src.at[at], dst.at[at])
+        else:
+            dst[at, :] = src[at, :]
         return group
 
     def z_mix(src, dst, r0, r1_):
@@ -173,6 +186,8 @@
     core_a.recv()
     u[...] = (wide(loc, ...) * sign_c + wide(loc_in, ...)).astype(BF)
     za = [z_start(u, z_in, *rs) for rs in CHUNKS]
+    up_start(1)
+    up_start(3)
 
     def multiply(d):
         group = up[PLACE[d] : PLACE[d] + 256, :]
@@ -255,21 +270,21 @@
     def z_second(j):
         gz_cp[j].recv()
         z_mix(gz_in, gz_out, *CHUNKS[j])
-        gw_cp[j] = z_start(gz_out, mixed, *CHUNKS[j])
-
-    def add_grad(slots, r0, r1_, fresh):
+        gw_cp[j] = z_start(gz_out, mixed_hbm, *CHUNKS[j])
+
+    def grad_step(slots, fresh=False):
         tokens = slice(slots[0] * HB, (slots[-1] + 1) * HB)
-
-        @pl.loop(0, 2)
-        def _(i):
-            columns = rows(i * 512, 512, 512)
-            block = jnp.concatenate([rot[k, r0:r1_, :] for k in slots], axis=1)
-            term = jnp.dot(block, up[tokens, columns], preferred_element_type=F32)
-            acc[r0:r1_, columns] = term if fresh else acc[r0:r1_, columns] + term
-
-    def grad_step(slots, fresh=False):
-        for r0, r1_ in OUT_ROWS:
-            add_grad(slots, r0, r1_, fresh)
+        for r0, r1_ in ((0, W // 2), (W // 2, W)):
+
+            @pl.loop(0, 2)
+            def _(i):
+                columns = rows(i * 512, 512, 512)
+                block = jnp.concatenate([rot[k, r0:r1_, :] for k in slots], axis=1)
+                term = jnp.dot(block, up[tokens, columns], preferred_element_type=F32)
+                if fresh:
+                    acc[r0:r1_, columns] = term
+                else:
+                    acc_out[r0:r1_, columns] = (acc[r0:r1_, columns] + term).astype(BF)
 
     def slot(d, xr):
         return PLACE[d] // HB + xr
@@ -281,9 +296,9 @@
     def gather_second(cps, xr):
         top, low = pl.ds(0, W // 2), pl.ds(W // 2, W // 2)
         cps[0].recv()
-        one = send(rot.at[slot(3, xr), top], rot.at[slot(2, xr), top], y_dev(1))
+        one = send(rot.at[slot(3, xr), top], last_hbm.at[xr, top], y_dev(1))
         cps[1].recv()
-        two = send(rot.at[slot(1, xr), low], rot.at[slot(2, xr), low], y_dev(3))
+        two = send(rot.at[slot(1, xr), low], last_hbm.at[xr, low], y_dev(3))
         return [one, two]
 
     zb = []
@@ -314,6 +329,7 @@
     shared.recv()
     multiply(2)
     y_first(0)
+    store(up.at[pl.ds(PLACE[2], 256)], up_out)
     shared = share_up(1), share_up(3)
     shared[0].recv()
     shared[1].recv()
@@ -339,15 +355,43 @@
     near_cp = gather_first(0)
     x_second(1)
     z_second(0)
-    grad_step((0, 1), True)
+    last = gather_second(far_cp, 1)
     core_first(1)
     core_second(1)
-    last = gather_second(far_cp, 1)
+    grad_step((0, 1), True)
     z_second(1)
     last += gather_second(near_cp, 0)
     grad_step((2, 3, 4, 5))
+    store(acc_out, acc_hbm)
     gw_cp[0].recv()
     gw_cp[1].recv()
+    for cp in last:
+        cp.recv()
+    for cp in stores:
+        cp.wait()
+    for group in sent:
+        group.finish()
+
+
+def finish(
+    mixed_hbm, last_hbm, acc_hbm, up_hbm, w_hbm, sc_ref, mk_ref, rot_ref, s128_ref,
+    gh_hbm, gw_hbm, gs_hbm,
+    mixed, last, acc, up, w_v, first, gh_v, grad_v, gw_v, gs_v, sem,
+):
+    started = []
+
+    def copy(src, dst):
+        cp = pltpu.make_async_copy(src, dst, sem.at[len(started)])
+        started.append(cp)
+        cp.start()
+        return cp
+
+    head = copy(mixed_hbm, mixed), copy(last_hbm, last), copy(up_hbm, up)
+    loads = []
+    for r0, r1_ in OUT_ROWS:
+        at = pl.ds(r0, r1_ - r0)
+        loads.append((copy(acc_hbm.at[at], acc.at[at]), copy(w_hbm.at[at], w_v.at[at])))
+    head[0].wait()
     for k in range(NC):
         first[k] = lax.dot_general(
             mixed[k * HB : (k + 1) * HB, :], s128_ref[...], (((0,), (0,)), ((), ())),
@@ -357,47 +401,34 @@
     def store_gh(i, o, value):
         gh_v[rows(i * 32, 32, 32), o * HB : (o + 1) * HB] = value
 
-    mix_blocks(store_gh, lambda k, o: rot_ref[o, k])
-    gh_out = pltpu.make_async_copy(gh_v, gh_hbm, lsem.at[2])
-    gh_out.start()
-
-    for cp in last:
-        cp.recv()
-    outs = []
-    for i, (r0, r1_) in enumerate(OUT_ROWS):
-        add_grad((6, 7), r0, r1_, False)
+    mix_blocks(first, store_gh, lambda k, o: rot_ref[o, k])
+    out = [copy(gh_v, gh_hbm)]
+    head[1].wait()
+    head[2].wait()
+    for (r0, r1_), (one, two) in zip(OUT_ROWS, loads):
+        one.wait()
+
+        @pl.loop(0, 2)
+        def _(i):
+            columns = rows(i * 512, 512, 512)
+            block = jnp.concatenate([last[k, r0:r1_, :] for k in range(2)], axis=1)
+            term = jnp.dot(block, up[:, columns], preferred_element_type=F32)
+            grad_v[r0:r1_, columns] = term + acc[r0:r1_, columns].astype(F32)
+
+        two.wait()
 
         @pl.loop(r0 // HB, r1_ // HB)
         def _(k):
             group = rows(k * HB, HB, HB)
             one = pl.ds(k, 1)
             for at in (slice(0, 512), slice(512, 1024)):
-                grad = acc[group, at]
-                gs_ref[one, at] = jnp.sum(grad * w_v[group, at].astype(F32), axis=0, keepdims=True)
+                grad = grad_v[group, at]
+                gs_v[one, at] = jnp.sum(grad * w_v[group, at].astype(F32), axis=0, keepdims=True)
                 gw_v[group, at] = (grad * (sc_ref[one, at] * mk_ref[one, at].astype(F32))).astype(BF)
 
         done = pl.ds(r0, r1_ - r0)
-        outs.append(pltpu.make_async_copy(gw_v.at[done], gw_hbm.at[done], lsem.at[3 + i]))
-        outs[-1].start()
-    outs.append(pltpu.make_async_copy(gs_ref, gs_hbm, lsem.at[5]))
-    outs[-1].start()
-    for cp in outs:
-        cp.wait()
-    gh_out.wait()
-    for group in sent:
-        group.finish()
-
-
-def hand_over(gh, gw, gs, gh_out, gw_out, gs_out, gh_v, gw_v, gs_v, sem):
-    pieces = [(gw.at[at], gw_v.at[at], gw_out.at[at]) for at in (pl.ds(i * 208, 208) for i in range(8))]
-    pieces += [(gh, gh_v, gh_out), (gs, gs_v, gs_out)]
-    into = [pltpu.make_async_copy(a, b, sem.at[0, i]) for i, (a, b, _) in enumerate(pieces)]
-    out = [pltpu.make_async_copy(b, c, sem.at[1, i]) for i, (_, b, c) in enumerate(pieces)]
-    for cp in into:
-        cp.start()
-    for first, then in zip(into, out):
-        first.wait()
-        then.start()
+        out.append(copy(gw_v.at[done], gw_hbm.at[done]))
+    out.append(copy(gs_v, gs_hbm))
     for cp in out:
         cp.wait()
 
@@ -412,39 +443,47 @@
         two = pltpu.VMEM((2, W, HB), BF)
         halves = pltpu.VMEM((2, W // 2, HB), BF)
         whole = pltpu.VMEM((W, E), BF)
+        first = pltpu.VMEM((NC, HB, HB), F32)
         scratch = [
-            pltpu.VMEM((HB, 8 * E), BF), whole, whole, pltpu.VMEM((8 * HB, E), BF), pltpu.VMEM((NC, HB, HB), F32),
-            full, full, full, full, full, full, two, full, pltpu.VMEM((8, W, HB), BF),
+            pltpu.VMEM((HB, 8 * E), BF), whole, whole, pltpu.VMEM((8 * HB, E), BF), first,
+            full, full, full, full, full, full, two, full, pltpu.VMEM((6, W, HB), BF),
             pltpu.VMEM((4, 2, W, HB), BF), two, pltpu.VMEM((2, 2, W, HB), BF), halves, halves, two,
-            full, full, full, full, full, full, pltpu.VMEM((HB, W), BF), pltpu.VMEM((W, E), F32), whole,
-            pltpu.VMEM((NC, E), F32), pltpu.SemaphoreType.DMA((N_SEM,)), pltpu.SemaphoreType.DMA((N_SEM,)), pltpu.SemaphoreType.DMA((8,)),
+            full, full, full, full, full, pltpu.VMEM((W, E), F32), whole,
+            pltpu.SemaphoreType.DMA((N_SEM,)), pltpu.SemaphoreType.DMA((N_SEM,)), pltpu.SemaphoreType.DMA((8,)),
         ]
-        shapes = (
-            jax.ShapeDtypeStruct((HB, W), BF),
-            jax.ShapeDtypeStruct((W, E), BF),
-            jax.ShapeDtypeStruct((NC, E), F32),
-        )
-        results = pl.pallas_call(
+        mixed, last, acc, up = pl.pallas_call(
             kernel,
-            name="fused",
-            out_shape=shapes,
-            in_specs=[vmem, anywhere, anywhere, vmem, vmem, smem, vmem],
-            out_specs=(anywhere,) * 3,
+            name="exchange",
+            out_shape=(
+                jax.ShapeDtypeStruct((W, HB), BF),
+                jax.ShapeDtypeStruct((2, W, HB), BF),
+                jax.ShapeDtypeStruct((W, E), BF),
+                jax.ShapeDtypeStruct((2 * HB, E), BF),
+            ),
+            in_specs=[vmem, anywhere, anywhere, vmem, smem, vmem],
+            out_specs=(anywhere,) * 4,
             scratch_shapes=scratch,
             compiler_params=pltpu.CompilerParams(
                 collective_id=0, has_side_effects=True, vmem_limit_bytes=56 * 2**20
             ),
-        )(hidden, upstream, weight, scales, clip_mask, rot_block, s128)
+        )(hidden, upstream, weight, scales, rot_block, s128)
         return pl.pallas_call(
-            hand_over,
-            name="hand_over",
-            out_shape=shapes,
-            in_specs=[anywhere] * 3,
+            finish,
+            name="finish",
+            out_shape=(
+                jax.ShapeDtypeStruct((HB, W), BF),
+                jax.ShapeDtypeStruct((W, E), BF),
+                jax.ShapeDtypeStruct((NC, E), F32),
+            ),
+            in_specs=[anywhere] * 5 + [vmem, vmem, smem, vmem],
             out_specs=(anywhere,) * 3,
             scratch_shapes=[
-                pltpu.VMEM((HB, W), BF), whole, pltpu.VMEM((NC, E), F32), pltpu.SemaphoreType.DMA((2, 10)),
+                full, two, whole, pltpu.VMEM((2 * HB, E), BF), whole, first,
+                pltpu.VMEM((HB, W), BF), pltpu.VMEM((W, E), F32), whole, pltpu.VMEM((NC, E), F32),
+                pltpu.SemaphoreType.DMA((16,)),
             ],
-        )(*results)
+            compiler_params=pltpu.CompilerParams(vmem_limit_bytes=56 * 2**20),
+        )(mixed, last, acc, up, weight, scales, clip_mask, rot_block, s128)
 
     return jax.shard_map(
         step,

time: 91.9 us -> 90.9 us (0.989)
  no operation moved by 1% of the time
where the time goes in v3:
time: 90.9 us; the launch traced here: 90.7 us
  Pallas kernels  90.1 us (99%)
    pallas_call x1, Pallas kernels, step(): pl.pallas_call(kernel, name='exchange', out_shape=(jax.ShapeDtypeStruct((...  82.8 us
    pallas_call x1, Pallas kernels, step(): pl.pallas_call(finish, name='finish', out_shape=(jax.ShapeDtypeStruct((HB...  7.32 us

profile of v3, /device:TPU:1, one launch (start us, length us, event | category | flops | bytes accessed | tf_op | source)
XLA Modules:
  0.0 90.7 jit_solution(7104833316850377373)
XLA Ops:
  0.6 82.8 %exchange.1 = (bf16[1664,128]{1,0:T(8,128)(2,1)}, bf16[2,1664,128]{2,1,0:T(8,128)(2,1)}, bf16[1664,1024]{1,0:T(8,128)(2,1)}, bf16[256,1024]{1,0:T(8,128)(2,1)}) custom-call(bf16[128,1664]{1,0:T(8,128)(2,1)} %h_ref.1, bf16[128,8192]{1,0:T(8,128)(2,1)} %up_hbm.1, bf16[1664,1024]{1,0:T(8,128)(2,1)} %w_hbm.3, f32[13,1024]{1,0:T(8,128)} %sc_ref.3, ...), custom_call_target="tpu_custom_call" | custom-call | tf_op jit(solution)/shard_map/exchange/pallas_call | solution.py:454
  83.4 7.3 %finish.1 = (bf16[128,1664]{1,0:T(8,128)(2,1)}, bf16[1664,1024]{1,0:T(8,128)(2,1)}, f32[13,1024]{1,0:T(8,128)}) custom-call(bf16[1664,128]{1,0:T(8,128)(2,1)} %get-tuple-element.7.mixed_hbm, bf16[2,1664,128]{2,1,0:T(8,128)(2,1)} %get-tuple-element.8.last_hbm, bf16[1664,1024]{1,0:T(8,128)(2,1)} %get-tuple-element.9.acc_hbm, ...), custom_call_target="tpu_custom_call" | custom-call | tf_op jit(solution)/shard_map/finish/pallas_call | solution.py:470
